TPU v7x, 32 devices: a whole 2x2x4 slice. The times are simulated.
32 devices in a mesh: grp: 4 (over x, core), dp: 8 (over z, y).
Axes of the slice: x: 2, y: 2, z: 4, core: 2. Of those that a mesh axis runs over, the one named last changes fastest.
Arguments:
- normed: bfloat16 [16384, 1280], P(('grp', 'dp')), may hold values from -6 to 6
- w_in: bfloat16 [5120, 1280], replicated, may hold values from -0.15625 to 0.15625
- w_out: bfloat16 [1280, 2560], replicated, may hold values from -0.125 to 0.125
- cotangent: bfloat16 [16384, 1280], P(('grp', 'dp')), may hold values from -6 to 6
Outputs:
- grad_in: float32 [5120, 1280], P('dp')
- grad_out: float32 [1280, 2560], P('dp')
- grad_normed: bfloat16 [16384, 1280], P(('grp', 'dp'))
All inputs are finite; a program needn't handle non-finite values.
Results may differ from a plain program's by a relative error of at most 0.005.
Values sent between devices are 32-bit elements; how exact they have to be, the bound alone decides.
A program may use at most 192 MiB of HBM per device.

v0:
```python
import jax
import jax.numpy as jnp
from jax import lax
from jax.sharding import PartitionSpec as P


def cross_dot(left, right):
    return lax.dot_general(
        left, right, (((0,), (0,)), ((), ())), preferred_element_type=jnp.float32
    )


def local(normed, w_in, w_out, cotangent):
    width = w_out.shape[1]
    inner = lax.axis_size("dp")
    outer = lax.axis_size("grp")
    factor = (normed.shape[0] * inner * outer) ** (-0.5)
    proj = lax.dot_general(
        normed, w_in, (((1,), (1,)), ((), ())), preferred_element_type=jnp.float32
    )
    value = proj[:, :width]
    gate = proj[:, width:]
    cdf = 0.5 * (1.0 + lax.erf(gate * 2.0 ** (-0.5)))
    density = jnp.exp(-0.5 * gate * gate) * (2.0 * jnp.pi) ** (-0.5)
    act = (value * gate * cdf).astype(jnp.bfloat16)
    dact = jnp.dot(cotangent, w_out, preferred_element_type=jnp.float32)
    d_value = dact * gate * cdf
    d_gate = dact * value * (cdf + gate * density)
    dproj = jnp.concatenate([d_value, d_gate], axis=1).astype(jnp.bfloat16)
    grad_normed = jnp.dot(dproj, w_in, preferred_element_type=jnp.float32).astype(jnp.bfloat16)
    columns = dproj
    piece_in = lax.psum_scatter(
        cross_dot(columns, normed) * factor, "dp", scatter_dimension=0, tiled=True
    )
    columns = cotangent
    piece_out = lax.psum_scatter(
        cross_dot(columns, act) * factor, "dp", scatter_dimension=0, tiled=True
    )
    grad_in, grad_out = lax.psum((piece_in, piece_out), "grp")
    return (grad_in, grad_out, grad_normed)


def solution(mesh):
    placed = (P(("grp", "dp"), None), P(), P(), P(("grp", "dp"), None))
    return jax.shard_map(
        local,
        mesh=mesh,
        in_specs=placed,
        out_specs=(P("dp", None), P("dp", None), P(("grp", "dp"), None)),
        check_vma=False,
    )
```

profile of v0, /device:TPU:1, one launch (start us, length us, event | category | flops | bytes accessed | tf_op | source)
XLA Modules:
  0.0 811.1 jit_solution(7212171633218094981)
XLA Ops:
  7.2 0.0 copy-start
  7.2 0.0 copy-start.2
  7.2 0.0 reduce-scatter.7.cloned.1.call-start
  7.2 1.3 copy-done
  8.5 12.4 %fusion.11 = f32[512,5120]{1,0:T(8,128)} fusion(bf16[512,1280]{1,0:T(8,128)(2,1)S(1)} %copy-done, bf16[5120,1280]{1,0:T(8,128)(2,1)} %param.5), kind=kOutput, calls=%fused_computation.18 | convolution fusion | flops 6710886400 | bytes 24903680 | tf_op jit(solution)/shard_map/dot_general | solution.py:18
  20.9 0.0 copy-done.2
  20.9 9.2 %fusion = f32[1280,2560]{0,1:T(8,128)} fusion(bf16[512,1280]{1,0:T(8,128)(2,1)S(1)} %copy-done.2, f32[512,5120]{1,0:T(8,128)} %fusion.11), kind=kOutput, calls=%fused_computation.2 | convolution fusion | flops 3366584320 | bytes 24903680 | tf_op jit(solution)/shard_map/dot_general | solution.py:8
  30.0 13.9 %copy.9 = f32[1280,2560]{1,0:T(8,128)} copy(f32[1280,2560]{0,1:T(8,128)} %fusion) | data formatting | bytes 26214400
  43.9 0.0 reduce-scatter.7.cloned.1.call-update
  44.0 0.0 reduce-scatter.5.cloned.1.call-start
  44.0 8.6 %multiply_convert_fusion.1 = (bf16[512,2560]{1,0:T(8,128)(2,1)S(1)}, bf16[512,2560]{1,0:T(8,128)(2,1)S(1)}) fusion(f32[512,5120]{1,0:T(8,128)} %fusion.11, bf16[512,1280]{1,0:T(8,128)(2,1)S(1)} %copy-done.2, bf16[1280,2560]{1,0:T(8,128)(2,1)} %param.6), kind=kOutput, calls=%fused_computation.12 | convolution fusion | flops 3373793280 | bytes 23592960 | tf_op jit(solution)/shard_map/dot_general | solution.py:26
  52.7 0.0 copy-start.3
  52.7 0.0 copy-start.4
  52.7 1.6 copy-done.3
  54.3 1.3 copy-done.4
  55.6 12.4 %convolution_multiply_fusion = f32[5120,1280]{1,0:T(8,128)} fusion(bf16[512,1280]{1,0:T(8,128)(2,1)S(1)} %copy-done, bf16[512,2560]{1,0:T(8,128)(2,1)S(1)} %get-tuple-element.12, bf16[512,2560]{1,0:T(8,128)(2,1)S(1)} %get-tuple-element.11), kind=kOutput, calls=%fused_computation | convolution fusion | flops 6727925760 | bytes 32768000 | tf_op jit(solution)/shard_map/dot_general | solution.py:8
  67.9 0.0 reduce-scatter.5.cloned.1.call-update
  68.0 0.2 all-reduce.3.cloned.1.call-start
  68.2 192.6 %reduce-scatter.7.cloned.1.call-done = f32[160,2560]{1,0:T(8,128)} async-done(((f32[1280,2560]{1,0:T(8,128)}), f32[160,2560]{1,0:T(8,128)}) %reduce-scatter.7.cloned.1.call-update) | async-done | bytes 1638416
  260.8 3.0 copy.10
  263.8 418.3 %reduce-scatter.5.cloned.1.call-done = f32[640,1280]{1,0:T(8,128)} async-done(((f32[5120,1280]{1,0:T(8,128)}), f32[640,1280]{1,0:T(8,128)}) %reduce-scatter.5.cloned.1.call-update) | async-done | bytes 3276816 | tf_op jit(solution)/shard_map/reduce_scatter | solution.py:32
  682.1 0.0 all-reduce.3.cloned.1.call-update
  682.1 13.5 %fusion.8 = bf16[512,1280]{1,0:T(8,128)(2,1)} fusion(bf16[5120,1280]{1,0:T(8,128)(2,1)} %param.5, bf16[512,2560]{1,0:T(8,128)(2,1)} %copy-done.4, bf16[512,2560]{1,0:T(8,128)(2,1)} %copy-done.3), kind=kOutput, calls=%fused_computation.15 | convolution fusion | flops 6722027520 | bytes 19660800 | tf_op jit(solution)/shard_map/dot_general | solution.py:30
  695.6 102.0 %all-reduce.3.cloned.1.call-done = (f32[640,1280]{1,0:T(8,128)}, f32[160,2560]{0,1:T(8,128)}) async-done(((f32[640,1280]{1,0:T(8,128)}, f32[160,2560]{0,1:T(8,128)}), (f32[640,1280]{1,0:T(8,128)}, f32[160,2560]{0,1:T(8,128)})) %all-reduce.3.cloned.1.call-update) | async-done | bytes 4915216 | tf_op jit(solution)/shard_map/psum | solution.py:39
  797.6 0.0 copy-start.1
  797.6 3.1 copy.8
  800.7 3.8 copy.13
  804.5 0.0 copy-done.1
Async XLA Ops:
  7.2 1.3 copy-start
  7.2 13.7 %copy-start.2 = (bf16[512,1280]{1,0:T(8,128)(2,1)S(1)}, bf16[512,1280]{1,0:T(8,128)(2,1)}, u32[]{:S(2)}) copy-start(bf16[512,1280]{1,0:T(8,128)(2,1)} %param.7) | copy-start | bytes 3932164
  7.2 253.6 %reduce-scatter.7.cloned.1.call-start = ((), (), s32[]{:S(2)}) async-start(), calls=%async_computation.3 | async-start | bytes 14745600
  44.0 638.1 %reduce-scatter.5.cloned.1.call-start = ((), (), s32[]{:S(2)}) async-start(), calls=%async_computation.2 | async-start | bytes 29491200 | tf_op jit(solution)/shard_map/reduce_scatter | solution.py:32
  52.7 1.6 copy-start.3
  52.7 2.9 copy-start.4
  68.0 729.6 %all-reduce.3.cloned.1.call-start = ((), (), s32[]{:S(2)}) async-start(), calls=%async_computation.4 | async-start | bytes 11796480 | tf_op jit(solution)/shard_map/psum | solution.py:39
  797.6 6.9 copy-start.1
Sparse Core Ops, SparseCore 0:
  44.1 216.6 reduce-scatter.6
  264.7 417.3 reduce-scatter.4
  685.4 112.1 all-reduce.2
where the time goes:
time: 812 us; the launch traced here: 811 us
  waiting for transfers between devices  713 us (88%)
  matrix products  56 us (7%)
  local copies, waits for them, and re-layouts  28 us (3%)
  between operations  13.8 us (2%)
    reduce_scatter x1, waiting for transfers between devices, local(): lax.psum_scatter(cross_dot(columns, normed) * factor, 'dp', scatter_dimen...  418 us
    unnamed x4, waiting for transfers between devices  193 us
    psum x1, waiting for transfers between devices, local(): grad_in, grad_out = lax.psum((piece_in, piece_out), 'grp')  102 us
    unnamed x14, local copies, waits for them, and re-layouts  28 us
    dot_general x2, matrix products, cross_dot(): lax.dot_general(left, right, (((0,), (0,)), ((), ())), preferred_element_...  21.5 us
  transfers between devices with their start and end apart: 3, of which 3 were waited for; matrix products, arithmetic and copies ran while one was open for 5% of the time, Pallas kernels for 0%

commit v1 on v0

v1 whole, which is shorter than its diff:
```python
import functools

import jax
import jax.numpy as jnp
from jax import lax
from jax.experimental import pallas as pl
from jax.experimental.pallas import tpu as pltpu
from jax.sharding import PartitionSpec as P

MESH = pl.DeviceIdType.MESH


def greet(partners):
    barrier = pltpu.get_barrier_semaphore()
    for partner in partners:
        pl.semaphore_signal(barrier, inc=1, device_id=partner, device_id_type=MESH)
    pl.semaphore_wait(barrier, len(partners))


def trade_kernel(normed, cot, all_normed, all_cot, mine, theirs, send_sem, recv_sem):
    grp = lax.axis_index("grp")
    dp = lax.axis_index("dp")
    other = (grp + 1 - 2 * lax.rem(grp, 2), dp)
    rows = normed.shape[0]
    mine[0] = normed[...].astype(jnp.float32)
    mine[1] = cot[...].astype(jnp.float32)
    greet([other])
    copies = [
        pltpu.make_async_remote_copy(
            src_ref=mine.at[k], dst_ref=theirs.at[k], send_sem=send_sem.at[k],
            recv_sem=recv_sem.at[k], device_id=other, device_id_type=MESH,
        )
        for k in range(2)
    ]
    for copy in copies:
        copy.start()
    all_normed[:rows] = normed[...]
    all_cot[:rows] = cot[...]
    copies[0].wait_recv()
    all_normed[rows:] = theirs[0].astype(jnp.bfloat16)
    copies[1].wait_recv()
    all_cot[rows:] = theirs[1].astype(jnp.bfloat16)
    for copy in copies:
        copy.wait_send()


def trade(normed, cot):
    rows, width = normed.shape
    whole = jax.ShapeDtypeStruct((2 * rows, width), jnp.bfloat16)
    vmem = pl.BlockSpec(memory_space=pltpu.VMEM)
    return pl.pallas_call(
        trade_kernel,
        out_shape=(whole, whole),
        in_specs=[vmem, vmem],
        out_specs=(vmem, vmem),
        scratch_shapes=[
            pltpu.VMEM((2, rows, width), jnp.float32),
            pltpu.VMEM((2, rows, width), jnp.float32),
            pltpu.SemaphoreType.DMA((2,)),
            pltpu.SemaphoreType.DMA((2,)),
        ],
        compiler_params=pltpu.CompilerParams(
            collective_id=0, has_side_effects=True, vmem_limit_bytes=40 * 2**20
        ),
        name="trade_tokens",
    )(normed, cot)


def sum_kernel(
    n, factor, dprojt, normed, cott, actt, out_r, out_x,
    part_r, part_x, land_r, land_e, land_x, final_r, land_p,
    ring_r, ring_x, halves, pair_r, core_r, spread,
):
    grp = lax.axis_index("grp")
    dp = lax.axis_index("dp")
    x, core = grp // 2, lax.rem(grp, 2)
    half = n // 2
    up = lax.rem(dp, 2)
    pos = jnp.where(up == 0, dp // 2, n - 1 - dp // 2)

    def member(place):
        place = lax.rem(place + 2 * n, n)
        return jnp.where(place < half, 2 * place, 2 * (n - 1 - place) + 1)

    following, previous = (grp, member(pos + 1)), (grp, member(pos - 1))
    along_x = ((1 - x) * 2 + core, dp)
    other = (x * 2 + 1 - core, dp)
    greet([following, previous, along_x, other])
    onward = (following, previous)

    go = cott.shape[1]
    rows_r = part_r.shape[2]
    rows_h = part_x.shape[3]
    cols = part_r.shape[3]
    split = rows_r - go

    def dot(left, right, axis):
        return lax.dot_general(
            left, right, (((1,), (axis,)), ((), ())), preferred_element_type=jnp.float32
        )

    def owner(way, s):
        return member(pos - 1 - s) if way == 0 else member(pos + 1 + s)

    def compute_r(s):
        for way in range(2):
            d = owner(way, s)
            span = slice(way * cols, (way + 1) * cols)
            part_r[way, s, :go] = dot(cott[d], actt[span, :], 1)
            part_r[way, s, go:] = dot(dprojt[d, :split], normed[:, span], 0)

    def compute_x(s):
        for way in range(2):
            d = owner(way, s)
            span = slice(way * cols, (way + 1) * cols)
            term = dot(dprojt[d, split:], normed[:, span], 0)
            part_x[0, s, way] = term[:rows_h]
            part_x[1, s, way] = term[rows_h:]

    def remote(src, dst, sems, where, device):
        return pltpu.make_async_remote_copy(
            src_ref=src, dst_ref=dst, send_sem=sems.at[(0,) + where],
            recv_sem=sems.at[(1,) + where], device_id=device, device_id_type=MESH,
        )

    def hop_r(way, s, first=False):
        src = part_r.at[way, 0] if first else land_r.at[way, s - 1]
        return remote(src, land_r.at[way, s], ring_r, (way, s), onward[way])

    def hop_x(way, s, first=False):
        src = land_e.at[0, way] if first else land_x.at[way, s - 1]
        return remote(src, land_x.at[way, s], ring_x, (way, s), onward[way])

    def give_half(s):
        return remote(part_x.at[1 - x, s], land_e.at[s], halves, (s,), along_x)

    def loop(first, last, body):
        def step(s, carry):
            body(s)
            return carry

        lax.fori_loop(first, last, step, 0)

    compute_r(0)
    for way in range(2):
        hop_r(way, 0, True).start()

    def make_x(s):
        compute_x(s)
        give_half(s).start()

    loop(0, n, make_x)
    loop(1, n, compute_r)

    def step_r(s):
        for way in range(2):
            hop_r(way, s, True).wait_recv()
            land_r[way, s] = land_r[way, s] + part_r[way, s + 1]
            hop_r(way, s + 1).start()

    def step_x(s):
        give_half(s + 1).wait_recv()
        for way in range(2):
            hop_x(way, s, True).wait_recv()
            land_x[way, s] = land_x[way, s] + (part_x[x, s + 1, way] + land_e[s + 1, way])
            hop_x(way, s + 1).start()

    def step_both(s):
        step_r(s)
        step_x(s - lag)

    lag = min(n // 2, n - 2)
    loop(0, lag, step_r)
    give_half(0).wait_recv()
    for way in range(2):
        land_e[0, way] = land_e[0, way] + part_x[x, 0, way]
        hop_x(way, 0, True).start()
    loop(lag, n - 2, step_both)

    def swap_r(way):
        return remote(final_r.at[way], land_p.at[way], pair_r, (way,), along_x)

    def tell_r(way):
        return remote(out_r.at[core, way], out_r.at[core, way], core_r, (way,), other)

    def hear_r(way):
        return remote(out_r.at[1 - core, way], out_r.at[1 - core, way], core_r, (way,), other)

    for way in range(2):
        hop_r(way, n - 2, True).wait_recv()
        final_r[way] = (land_r[way, n - 2] + part_r[way, n - 1]) * factor
        swap_r(way).start()

    loop(n - 2 - lag, n - 2, step_x)

    def show(which, c, h, way, device):
        spot = out_x.at[c, h, way]
        return remote(spot, spot, spread, (which, way), device)

    give_half(n - 1).wait_recv()
    for way in range(2):
        hop_x(way, n - 2, True).wait_recv()
        out_x[core, x, way] = (
            land_x[way, n - 2] + (part_x[x, n - 1, way] + land_e[n - 1, way])
        ) * factor
        show(0, core, x, way, along_x).start()
        show(1, core, x, way, other).start()
    for way in range(2):
        swap_r(way).wait_recv()
        out_r[core, way] = final_r[way] + land_p[way]
        tell_r(way).start()
    for way in range(2):
        show(0, core, 1 - x, way, along_x).wait_recv()
        show(2, core, 1 - x, way, other).start()
    for way in range(2):
        hear_r(way).wait_recv()
        show(1, 1 - core, x, way, other).wait_recv()
        show(2, 1 - core, 1 - x, way, other).wait_recv()

    def drain(s):
        for way in range(2):
            hop_r(way, s, True).wait_send()
            hop_x(way, s, True).wait_send()

    loop(0, n - 1, drain)
    loop(0, n, lambda s: give_half(s).wait_send())
    for way in range(2):
        swap_r(way).wait_send()
        tell_r(way).wait_send()
        show(0, core, x, way, along_x).wait_send()
        show(1, core, x, way, other).wait_send()
        show(2, core, 1 - x, way, other).wait_send()


def sum_all(n, factor, dprojt, normed, cott, actt):
    gi, go, width = dprojt.shape[1], cott.shape[1], normed.shape[1]
    rows = gi + go
    rows_x = rows * 7 // 15 // 32 * 32
    rows_r, rows_h, cols = rows - rows_x, rows_x // 2, width // 2
    vmem = pl.BlockSpec(memory_space=pltpu.VMEM)
    f32 = jnp.float32
    dma = pltpu.SemaphoreType.DMA
    tokens = normed.shape[0]
    return pl.pallas_call(
        functools.partial(sum_kernel, n, factor),
        out_shape=(
            jax.ShapeDtypeStruct((2, 2, rows_r, cols), f32),
            jax.ShapeDtypeStruct((2, 2, 2, rows_h, cols), f32),
        ),
        in_specs=[vmem] * 4,
        out_specs=(vmem, vmem),
        scratch_shapes=[
            pltpu.VMEM((2, n, rows_r, cols), f32),
            pltpu.VMEM((2, n, 2, rows_h, cols), f32),
            pltpu.VMEM((2, n - 1, rows_r, cols), f32),
            pltpu.VMEM((n, 2, rows_h, cols), f32),
            pltpu.VMEM((2, n - 1, rows_h, cols), f32),
            pltpu.VMEM((2, rows_r, cols), f32),
            pltpu.VMEM((2, rows_r, cols), f32),
            dma((2, 2, n - 1)),
            dma((2, 2, n - 1)),
            dma((2, n)),
            dma((2, 2)),
            dma((2, 2)),
            dma((2, 3, 2)),
        ],
        compiler_params=pltpu.CompilerParams(
            collective_id=1, has_side_effects=True, vmem_limit_bytes=62 * 2**20
        ),
        cost_estimate=pl.CostEstimate(
            flops=2 * n * rows * tokens * width, bytes_accessed=20 * 2**20, transcendentals=0
        ),
        name="sum_gradients",
    )(dprojt, normed, cott, actt)


def local(normed, w_in, w_out, cotangent):
    width = w_out.shape[1]
    model = w_in.shape[1]
    n = lax.axis_size("dp")
    outer = lax.axis_size("grp")
    tokens = normed.shape[0]
    factor = (tokens * n * outer) ** (-0.5)
    core = lax.rem(lax.axis_index("grp"), 2)
    gi = 2 * width // n // 2
    go = model // n
    units = width // 2

    w_in_c = lax.dynamic_index_in_dim(
        w_in.reshape(n, 2, gi, model), core, 1, keepdims=False
    ).reshape(2 * units, model)
    w_out_c = lax.dynamic_index_in_dim(
        w_out.reshape(model, n // 2, 2, gi), core, 2, keepdims=False
    ).reshape(model, units)

    both, both_cot = trade(normed, cotangent)
    projt = lax.dot_general(
        w_in_c, both, (((1,), (1,)), ((), ())), preferred_element_type=jnp.float32
    )
    value, gate = projt[:units], projt[units:]
    cdf = 0.5 * (1.0 + lax.erf(gate * 2.0 ** (-0.5)))
    density = jnp.exp(-0.5 * gate * gate) * (2.0 * jnp.pi) ** (-0.5)
    actt = (value * gate * cdf).astype(jnp.bfloat16)
    dactt = lax.dot_general(
        w_out_c, both_cot, (((0,), (1,)), ((), ())), preferred_element_type=jnp.float32
    )
    d_value = dactt * gate * cdf
    d_gate = dactt * value * (cdf + gate * density)
    dprojt = jnp.concatenate([d_value, d_gate], axis=0).astype(jnp.bfloat16)

    share = lax.dot_general(
        dprojt, w_in_c, (((0,), (0,)), ((), ())), preferred_element_type=jnp.float32
    )
    pairs = [(i, i + 1 - 2 * (i % 2)) for i in range(outer)]
    came = lax.ppermute(share[tokens:], "grp", pairs)
    grad_normed = (share[:tokens] + came).astype(jnp.bfloat16)

    sum_r, sum_x = sum_all(
        n, factor, dprojt.reshape(n, gi, 2 * tokens), both,
        both_cot.T.reshape(n, go, 2 * tokens), actt,
    )
    rows_r = sum_r.shape[2]
    wide_r = sum_r.transpose(0, 2, 1, 3).reshape(2, rows_r, model)
    wide_x = sum_x.transpose(0, 1, 3, 2, 4).reshape(2, -1, model)
    grad_in = jnp.concatenate([wide_r[:, go:], wide_x], axis=1).reshape(2 * gi, model)
    grad_out = (
        wide_r[:, :go].reshape(2, go, n // 2, gi).transpose(1, 2, 0, 3).reshape(go, width)
    )
    return (grad_in, grad_out, grad_normed)


def solution(mesh):
    placed = (P(("grp", "dp"), None), P(), P(), P(("grp", "dp"), None))
    return jax.shard_map(
        local,
        mesh=mesh,
        in_specs=placed,
        out_specs=(P("dp", None), P("dp", None), P(("grp", "dp"), None)),
        check_vma=False,
    )
```

time: 812 us -> 277 us (0.34)
  waiting for transfers between devices: 713 us -> 0.01 us
  Pallas kernels: 0 us -> 186 us
  matrix products: 56 us -> 24.4 us
  local copies, waits for them, and re-layouts: 28 us -> 48.3 us
  other arithmetic: 0 us -> 16.9 us
  between operations: 13.8 us -> 0.77 us
    reduce_scatter x1 -> x0, waiting for transfers between devices: 418 us -> none  [local(): lax.psum_scatter(cross_dot(columns, normed) * factor, 'dp', scatter_dimen...]
    unnamed x4 -> x0, waiting for transfers between devices: 193 us -> none
    pallas_call x0 -> x2, Pallas kernels: none -> 186 us  [the longest x1 177 us: sum_all(): pl.pallas_call(functools.partial(sum_kernel, n, factor), out_shape=(jax.S...]
    psum x1 -> x0, waiting for transfers between devices: 102 us -> none  [local(): grad_in, grad_out = lax.psum((piece_in, piece_out), 'grp')]
    dot_general x5 -> x3, matrix products: 56 us -> 24.4 us  [the longest x1 10.3 us: local(): lax.dot_general(dprojt, w_in_c, (((0,), (0,)), ((), ())), preferred_eleme...]
    convert_element_type x0 -> x3, other arithmetic: none -> 15 us  [the longest x1 5.82 us: local(): actt = (value * gate * cdf).astype(jnp.bfloat16)]
    unnamed x14 -> x21, local copies, waits for them, and re-layouts: 28 us -> 13.1 us
    transpose x0 -> x4, local copies, waits for them, and re-layouts: none -> 13.6 us  [the longest x1 4.47 us: local(): wide_r[:, :go].reshape(2, go, n // 2, gi).transpose(1, 2, 0, 3)]
  transfers between devices with their start and end apart: 3 -> 1, of which waited for: 3 -> 0; matrix products, arithmetic and copies ran while one was open for 5% -> 15% of each run, Pallas kernels for 0% -> 64%
where the time goes in v1:
time: 277 us
  Pallas kernels  186 us (67%)
  local copies, waits for them, and re-layouts  48.3 us (17%)
  matrix products  24.4 us (9%)
  other arithmetic  16.9 us (6%)
    pallas_call x1, Pallas kernels, sum_all(): pl.pallas_call(functools.partial(sum_kernel, n, factor), out_shape=(jax.S...  177 us
    unnamed x21, local copies, waits for them, and re-layouts  13.1 us
    dot_general x1, matrix products, local(): lax.dot_general(dprojt, w_in_c, (((0,), (0,)), ((), ())), preferred_eleme...  10.3 us
    pallas_call x1, Pallas kernels, trade(): pl.pallas_call(trade_kernel, out_shape=(whole, whole), in_specs=[vmem, vm...  9.16 us
    dot_general x1, matrix products, local(): lax.dot_general(w_out_c, both_cot, (((0,), (1,)), ((), ())), preferred_el...  7.11 us
    dot_general x1, matrix products, local(): lax.dot_general(w_in_c, both, (((1,), (1,)), ((), ())), preferred_element...  7.01 us
    reshape x2, local copies, waits for them, and re-layouts, local(): wide_r[:, :go].reshape(2, go, n // 2, gi).transpose(1, 2, 0, 3)  6.37 us
    convert_element_type x1, other arithmetic, local(): actt = (value * gate * cdf).astype(jnp.bfloat16)  5.82 us
  transfers between devices with their start and end apart: 1, of which 0 were waited for; matrix products, arithmetic and copies ran while one was open for 15% of the time, Pallas kernels for 64%

profile of v1, /device:TPU:1, one launch (start us, length us, event | category | flops | bytes accessed | tf_op | source)
XLA Modules:
  0.0 276.7 jit_solution(1496329960240964801)
XLA Ops:
  0.6 9.5 %copy.14 = bf16[1280,2560]{0,1:T(8,128)(2,1)} copy(bf16[1280,2560]{1,0:T(8,128)(2,1)} %param.6) | data formatting | bytes 13107200 | tf_op args[2]
  10.1 3.5 %constant_dynamic-slice_fusion = bf16[8,1,320,1280]{3,2,1,0:T(8,128)(2,1)S(1)} fusion(bf16[8,2,320,1280]{3,2,1,0:T(8,128)(2,1)} %bitcast.27, s32[]{:T(128)S(6)} %select_n.6), kind=kLoop, calls=%fused_computation.13 | loop fusion | bytes 13107204 | tf_op jit(solution)/shard_map/jit(dynamic_index_in_dim)/dynamic_slice | solution.py:289
  13.6 0.0 copy-start
  13.6 0.0 copy-start.1
  13.6 1.2 copy-done.3
  14.9 1.9 constant_dynamic-slice_fusion.1
  16.8 0.0 copy-done
  16.8 0.0 copy-done.1
  16.8 9.2 %trade_tokens.1 = (bf16[1024,1280]{1,0:T(8,128)(2,1)S(1)}, bf16[1024,1280]{1,0:T(8,128)(2,1)S(1)}) custom-call(bf16[512,1280]{1,0:T(8,128)(2,1)S(1)} %copy-done, bf16[512,1280]{1,0:T(8,128)(2,1)S(1)} %copy-done.1), custom_call_target="tpu_custom_call" | custom-call | tf_op jit(solution)/shard_map/trade_tokens/pallas_call | solution.py:51
  26.0 0.0 copy-start.2
  26.0 0.0 copy-start.8
  26.0 7.0 %fusion.7 = f32[2560,1024]{1,0:T(8,128)S(1)} fusion(bf16[2560,1280]{1,0:T(8,128)(2,1)S(1)} %bitcast.24, bf16[1024,1280]{1,0:T(8,128)(2,1)S(1)} %get-tuple-element.8.normed), kind=kOutput, calls=%fused_computation.16 | convolution fusion | flops 6710886400 | bytes 19660800 | tf_op jit(solution)/shard_map/dot_general | solution.py:297
  33.0 7.1 %multiply_multiply_fusion.1 = (bf16[1280,1024]{1,0:T(8,128)(2,1)S(1)}, bf16[1280,1024]{1,0:T(8,128)(2,1)}) fusion(f32[2560,1024]{1,0:T(8,128)S(1)} %fusion.7, bf16[1280,1280]{0,1:T(8,128)(2,1)S(1)} %bitcast.29, bf16[1024,1280]{1,0:T(8,128)(2,1)S(1)} %get-tuple-element.7), kind=kOutput, calls=%fused_computation.9 | convolution fusion | flops 3373793280 | bytes 21626880 | tf_op jit(solution)/shard_map/dot_general | solution.py:304
  40.1 10.3 %fusion.6 = f32[1024,1280]{1,0:T(8,128)S(1)} fusion(bf16[2560,1280]{1,0:T(8,128)(2,1)S(1)} %bitcast.25, bf16[1280,1024]{1,0:T(8,128)(2,1)} %get-tuple-element.12, bf16[1280,1024]{1,0:T(8,128)(2,1)S(1)} %get-tuple-element.11), kind=kOutput, calls=%fused_computation.15 | convolution fusion | flops 6721372160 | bytes 17039360 | tf_op jit(solution)/shard_map/dot_general | solution.py:311
  50.4 2.3 copy-done.6
  52.8 1.7 slice.29
  54.5 0.1 collective-permute-start
  54.6 2.7 copy.15
  57.3 5.4 %maximum_convert_fusion = bf16[2560,1024]{1,0:T(8,128)(2,1)} fusion(bf16[1280,1024]{1,0:T(8,128)(2,1)} %get-tuple-element.12, bf16[1280,1024]{1,0:T(8,128)(2,1)} %copy-done.9), kind=kLoop, calls=%fused_computation | loop fusion | flops 10485760 | bytes 10485760 | tf_op jit(solution)/shard_map/convert_element_type | solution.py:309
  62.7 5.8 %multiply_convert_fusion.actt = bf16[1280,1024]{1,0:T(8,128)(2,1)} fusion(f32[2560,1024]{1,0:T(8,128)} %copy-done.4), kind=kLoop, calls=%fused_computation.7 | loop fusion | flops 7864320 | bytes 13107200 | tf_op jit(solution)/shard_map/convert_element_type | solution.py:303
  68.5 177.1 %sum_gradients.1 = (f32[2,2,256,640]{3,2,1,0:T(8,128)}, f32[2,2,2,112,640]{4,3,2,1,0:T(8,128)}) custom-call(bf16[8,320,1024]{2,1,0:T(8,128)(2,1)} %bitcast.26, bf16[1024,1280]{1,0:T(8,128)(2,1)} %copy-done.2, bf16[8,160,1024]{2,1,0:T(8,128)(2,1)} %bitcast.30, bf16[1280,1024]{1,0:T(8,128)(2,1)} %multiply_convert_fusion.actt), custom_call_target="tpu_custom_call" | custom-call | flops 10066329600 | bytes 20971520 | tf_op jit(solution)/shard_map/sum_gradients/pallas_call | solution.py:244
  245.5 2.2 copy.16
  247.7 1.5 slice.26
  249.2 2.7 copy.18
  251.9 4.2 %copy.17 = f32[2,2,112,2,640]{4,3,2,1,0:T(2,128)} copy(f32[2,2,112,2,640]{4,2,3,1,0:T(8,128)} %bitcast.32) | data formatting | bytes 4587520 | tf_op jit(solution)/shard_map/transpose | solution.py:324
  256.1 4.0 %reshape.47 = f32[2,224,1280]{2,1,0:T(8,128)} reshape(f32[2,2,112,2,640]{4,3,2,1,0:T(2,128)} %copy.17) | data formatting | bytes 4587520 | tf_op jit(solution)/shard_map/reshape | solution.py:324
  260.1 2.5 copy.21
  262.6 4.5 %copy.20 = f32[160,4,2,320]{3,2,1,0:T(2,128)} copy(f32[160,4,2,320]{3,1,0,2:T(4,128)} %bitcast.23) | data formatting | bytes 3276800 | tf_op jit(solution)/shard_map/transpose | solution.py:327
  267.1 3.9 %reshape.50 = f32[160,2560]{1,0:T(8,128)} reshape(f32[160,4,2,320]{3,2,1,0:T(2,128)} %copy.20) | data formatting | bytes 3276800 | tf_op jit(solution)/shard_map/reshape | solution.py:327
  271.0 1.9 pad_maximum_fusion
  272.9 0.0 collective-permute-done
  272.9 3.8 %fusion.5 = bf16[512,1280]{1,0:T(8,128)(2,1)} fusion(f32[512,1280]{1,0:T(8,128)} %collective-permute-done, f32[1024,1280]{1,0:T(8,128)} %copy-done.6), kind=kLoop, calls=%fused_computation.12 | loop fusion | flops 1310720 | bytes 6553600 | tf_op jit(solution)/shard_map/convert_element_type | solution.py:316
  (12 shorter events, 0.0 us)
Async XLA Ops:
  10.1 4.7 %copy-start.3 = (bf16[1280,2560]{0,1:T(8,128)(2,1)S(1)}, bf16[1280,2560]{0,1:T(8,128)(2,1)}, u32[]{:S(2)}) copy-start(bf16[1280,2560]{0,1:T(8,128)(2,1)} %copy.14) | copy-start | bytes 19660804
  13.6 3.2 %copy-start = (bf16[512,1280]{1,0:T(8,128)(2,1)S(1)}, bf16[512,1280]{1,0:T(8,128)(2,1)}, u32[]{:S(2)}) copy-start(bf16[512,1280]{1,0:T(8,128)(2,1)} %normed.1) | copy-start | bytes 3932164
  13.6 3.2 %copy-start.1 = (bf16[512,1280]{1,0:T(8,128)(2,1)S(1)}, bf16[512,1280]{1,0:T(8,128)(2,1)}, u32[]{:S(2)}) copy-start(bf16[512,1280]{1,0:T(8,128)(2,1)} %cot.1) | copy-start | bytes 3932164
  26.0 7.0 %copy-start.2 = (bf16[1024,1280]{1,0:T(8,128)(2,1)}, bf16[1024,1280]{1,0:T(8,128)(2,1)S(1)}, u32[]{:S(2)}) copy-start(bf16[1024,1280]{1,0:T(8,128)(2,1)S(1)} %get-tuple-element.8.normed) | copy-start | bytes 7864324
  26.0 7.1 %copy-start.8 = (bf16[1280,4,1,320]{0,3,2,1:T(8,128)(2,1)S(1)}, bf16[1280,4,1,320]{0,3,2,1:T(8,128)(2,1)}, u32[]{:S(2)}) copy-start(bf16[1280,4,1,320]{0,3,2,1:T(8,128)(2,1)} %constant_dynamic-slice_fusion.1) | copy-start | bytes 9830404
  33.0 7.1 %copy-start.4 = (f32[2560,1024]{1,0:T(8,128)}, f32[2560,1024]{1,0:T(8,128)S(1)}, u32[]{:S(2)}) copy-start(f32[2560,1024]{1,0:T(8,128)S(1)} %fusion.7) | copy-start | bytes 31457284
  40.1 10.3 %copy-start.9 = (bf16[1280,1024]{1,0:T(8,128)(2,1)}, bf16[1280,1024]{1,0:T(8,128)(2,1)S(1)}, u32[]{:S(2)}) copy-start(bf16[1280,1024]{1,0:T(8,128)(2,1)S(1)} %get-tuple-element.11) | copy-start | bytes 7864324
  50.4 2.4 copy-start.6
  54.5 218.4 %collective-permute-start = (f32[512,1280]{1,0:T(8,128)}, f32[512,1280]{1,0:T(8,128)}, u32[]{:S(2)}, u32[]{:S(2)}) collective-permute-start(f32[512,1280]{1,0:T(8,128)} %slice.29), channel_id=1, source_target_pairs={{0,8},{8,0},{16,24},{24,16},{1,9},{9,1},{17,25},{25,17},{2,10},{10... | collective-permute-start | bytes 7864328 | tf_op jit(solution)/shard_map/ppermute | solution.py:315
  262.6 8.3 %copy-start.5 = (f32[2,224,1280]{2,1,0:T(8,128)S(1)}, f32[2,224,1280]{2,1,0:T(8,128)}, u32[]{:S(2)}) copy-start(f32[2,224,1280]{2,1,0:T(8,128)} %reshape.47) | copy-start | bytes 6881284
  262.6 8.3 %copy-start.7 = (f32[2,96,1280]{2,1,0:T(8,128)S(1)}, f32[2,96,1280]{2,1,0:T(8,128)}, u32[]{:S(2)}) copy-start(f32[2,96,1280]{2,1,0:T(8,128)} %copy.18) | copy-start | bytes 2949124

commit v2 on v1

v2 whole, which is shorter than its diff:
```python
import functools

import jax
import jax.numpy as jnp
from jax import lax
from jax.experimental import pallas as pl
from jax.experimental.pallas import tpu as pltpu
from jax.sharding import PartitionSpec as P

MESH = pl.DeviceIdType.MESH


def greet(partners):
    barrier = pltpu.get_barrier_semaphore()
    for partner in partners:
        pl.semaphore_signal(barrier, inc=1, device_id=partner, device_id_type=MESH)
    pl.semaphore_wait(barrier, len(partners))


def trade_kernel(normed, cot, all_normed, all_cot, mine, theirs, send_sem, recv_sem):
    grp = lax.axis_index("grp")
    dp = lax.axis_index("dp")
    other = (grp + 1 - 2 * lax.rem(grp, 2), dp)
    rows = normed.shape[0]
    mine[0] = normed[...].astype(jnp.float32)
    mine[1] = cot[...].astype(jnp.float32)
    greet([other])
    copies = [
        pltpu.make_async_remote_copy(
            src_ref=mine.at[k], dst_ref=theirs.at[k], send_sem=send_sem.at[k],
            recv_sem=recv_sem.at[k], device_id=other, device_id_type=MESH,
        )
        for k in range(2)
    ]
    for copy in copies:
        copy.start()
    all_normed[:rows] = normed[...]
    all_cot[:rows] = cot[...]
    copies[0].wait_recv()
    all_normed[rows:] = theirs[0].astype(jnp.bfloat16)
    copies[1].wait_recv()
    all_cot[rows:] = theirs[1].astype(jnp.bfloat16)
    for copy in copies:
        copy.wait_send()


def trade(normed, cot):
    rows, width = normed.shape
    whole = jax.ShapeDtypeStruct((2 * rows, width), jnp.bfloat16)
    vmem = pl.BlockSpec(memory_space=pltpu.VMEM)
    return pl.pallas_call(
        trade_kernel,
        out_shape=(whole, whole),
        in_specs=[vmem, vmem],
        out_specs=(vmem, vmem),
        scratch_shapes=[
            pltpu.VMEM((2, rows, width), jnp.float32),
            pltpu.VMEM((2, rows, width), jnp.float32),
            pltpu.SemaphoreType.DMA((2,)),
            pltpu.SemaphoreType.DMA((2,)),
        ],
        compiler_params=pltpu.CompilerParams(
            collective_id=0, has_side_effects=True, vmem_limit_bytes=40 * 2**20
        ),
        name="trade_tokens",
    )(normed, cot)


def sum_kernel(
    n, factor, dprojt, normed, cott, actt, w_in, out_in, out_out, out_normed,
    part_r, part_e, land_r, land_e, land_x, final_r, land_p, land_o, share, land_s, w_now,
    ring_r, ring_x, halves, pair_r, core_r, core_o, spread, core_s, fetch,
):
    grp = lax.axis_index("grp")
    dp = lax.axis_index("dp")
    x, core = grp // 2, lax.rem(grp, 2)
    half = n // 2
    up = lax.rem(dp, 2)
    pos = jnp.where(up == 0, dp // 2, n - 1 - dp // 2)

    def member(place):
        place = lax.rem(place + 2 * n, n)
        return jnp.where(place < half, 2 * place, 2 * (n - 1 - place) + 1)

    following, previous = (grp, member(pos + 1)), (grp, member(pos - 1))
    along_x = ((1 - x) * 2 + core, dp)
    other = (x * 2 + 1 - core, dp)
    greet([following, previous, along_x, other])
    onward = (following, previous)

    gi, go = dprojt.shape[1], cott.shape[1]
    rows_r = part_r.shape[1]
    rows_h, cols = land_e.shape[2:]
    split = rows_r - go
    spans = (slice(0, cols), slice(cols, 2 * cols))

    def dot(left, right, axes):
        return lax.dot_general(
            left, right, (((axes[0],), (axes[1],)), ((), ())),
            preferred_element_type=jnp.float32,
        )

    def owner(way, s):
        return member(pos - 1 - s) if way == 0 else member(pos + 1 + s)

    def compute_r(way, s):
        d = owner(way, s)
        part_r[way, :go] = dot(cott[d], actt[spans[way], :], (1, 1))
        part_r[way, go:] = dot(dprojt[d, :split], normed[:, spans[way]], (1, 0))

    def rows_of_half(h):
        return pl.ds(pl.multiple_of(split + h * rows_h, 16), rows_h)

    def compute_x(way, s, h):
        d = owner(way, s)
        return dot(dprojt[d, rows_of_half(h)], normed[:, spans[way]], (1, 0))

    def remote(src, dst, sems, where, device):
        return pltpu.make_async_remote_copy(
            src_ref=src, dst_ref=dst, send_sem=sems.at[(0,) + where],
            recv_sem=sems.at[(1,) + where], device_id=device, device_id_type=MESH,
        )

    def hop_r(way, s, first=False):
        src = final_r.at[way] if first else land_r.at[way, s - 1]
        return remote(src, land_r.at[way, s], ring_r, (way, s), onward[way])

    def hop_x(way, s, first=False):
        src = land_e.at[0, way] if first else land_x.at[way, s - 1]
        return remote(src, land_x.at[way, s], ring_x, (way, s), onward[way])

    def give_half(s):
        return remote(part_e.at[s], land_e.at[s], halves, (s,), along_x)

    def loop(first, last, body):
        def step(s, carry):
            body(s)
            return carry

        lax.fori_loop(first, last, step, 0)

    for way in range(2):
        compute_r(way, 0)
        final_r[way] = part_r[way]
        hop_r(way, 0, True).start()

    def make_x(s):
        for way in range(2):
            part_e[s, way] = compute_x(way, s, 1 - x)
        give_half(s).start()

    loop(0, n, make_x)

    tokens = out_normed.shape[0]

    def add_share(d, k, total):
        copy = pltpu.make_async_copy(w_in.at[d], w_now, fetch)
        copy.start()
        copy.wait()
        rows = slice(k * tokens, (k + 1) * tokens)
        for span in spans:
            total[:, span] += dot(dprojt[d, :, rows], w_now[:, span], (0, 0))

    share[...] = jnp.zeros_like(share)
    loop(0, n, lambda d: add_share(d, 1, share))
    give_share = remote(share, land_s, core_s, (), other)
    give_share.start()

    def step_r(s):
        for way in range(2):
            compute_r(way, s + 1)
        for way in range(2):
            hop_r(way, s, True).wait_recv()
            land_r[way, s] = land_r[way, s] + part_r[way]
            hop_r(way, s + 1).start()

    def step_first(s):
        step_r(s)
        add_share(s, 0, land_s)

    def own_x(way, s):
        return compute_x(way, s, x) + land_e[s, way]

    def step_x(s):
        give_half(s + 1).wait_recv()
        for way in range(2):
            land_e[s + 1, way] = own_x(way, s + 1)
        for way in range(2):
            hop_x(way, s, True).wait_recv()
            land_x[way, s] = land_x[way, s] + land_e[s + 1, way]
            hop_x(way, s + 1).start()

    def step_both(s):
        step_r(s)
        step_x(s - lag)
        add_share(s, 0, land_s)

    lag = min(n // 2, n - 2)
    step_r(0)
    give_share.wait_recv()
    for d in (0, n - 2, n - 1):
        add_share(d, 0, land_s)
    loop(1, lag, step_first)
    give_half(0).wait_recv()
    for way in range(2):
        land_e[0, way] = own_x(way, 0)
        hop_x(way, 0, True).start()
    loop(lag, n - 2, step_both)

    out_normed[...] = land_s[...].astype(out_normed.dtype)

    def swap_r(way):
        return remote(part_r.at[way], land_p.at[way], pair_r, (way,), along_x)

    for way in range(2):
        compute_r(way, n - 1)
        hop_r(way, n - 2, True).wait_recv()
        part_r[way] = (land_r[way, n - 2] + part_r[way]) * factor
        swap_r(way).start()

    loop(n - 2 - lag, n - 2, step_x)

    def tell_r(c, way):
        spot = out_in.at[c, :split, spans[way]]
        return remote(spot, spot, core_r, (way,), other)

    def tell_o(way):
        return remote(final_r.at[way, :go], land_o.at[way], core_o, (way,), other)

    def show(which, c, h, way, device):
        rows = pl.ds(pl.multiple_of(split + h * rows_h, 8), rows_h)
        spot = out_in.at[c, rows, spans[way]]
        return remote(spot, spot, spread, (which, way), device)

    give_half(n - 1).wait_recv()
    for way in range(2):
        land_e[n - 1, way] = own_x(way, n - 1)
    rows_x = pl.ds(pl.multiple_of(split + x * rows_h, 8), rows_h)
    for way in range(2):
        hop_x(way, n - 2, True).wait_recv()
        out_in[core, rows_x, spans[way]] = (
            land_x[way, n - 2] + land_e[n - 1, way]
        ) * factor
        show(0, core, x, way, along_x).start()
        show(1, core, x, way, other).start()
    for way in range(2):
        swap_r(way).wait_recv()
        hop_r(way, 0, True).wait_send()
        final_r[way, :go] = part_r[way, :go] + land_p[way, :go]
        tell_o(way).start()
        out_in[core, :split, spans[way]] = part_r[way, go:] + land_p[way, go:]
        tell_r(core, way).start()
    for way in range(2):
        show(0, core, 1 - x, way, along_x).wait_recv()
        show(2, core, 1 - x, way, other).start()
    for way in range(2):
        tell_o(way).wait_recv()
    mine = jnp.concatenate([final_r[0, :go], final_r[1, :go]], axis=1)
    theirs = jnp.concatenate([land_o[0], land_o[1]], axis=1)
    first = jnp.where(core == 0, mine, theirs)
    second = jnp.where(core == 0, theirs, mine)
    out_out[...] = jnp.concatenate(
        [
            block[:, b * gi : (b + 1) * gi]
            for b in range(half)
            for block in (first, second)
        ],
        axis=1,
    )
    for way in range(2):
        tell_r(1 - core, way).wait_recv()
        show(1, 1 - core, x, way, other).wait_recv()
        show(2, 1 - core, 1 - x, way, other).wait_recv()

    def drain(s):
        for way in range(2):
            hop_r(way, s + 1).wait_send()
            hop_x(way, s, True).wait_send()

    loop(0, n - 2, drain)
    for way in range(2):
        hop_x(way, n - 2, True).wait_send()
    loop(0, n, lambda s: give_half(s).wait_send())
    give_share.wait_send()
    for way in range(2):
        swap_r(way).wait_send()
        tell_o(way).wait_send()
        tell_r(core, way).wait_send()
        show(0, core, x, way, along_x).wait_send()
        show(1, core, x, way, other).wait_send()
        show(2, core, 1 - x, way, other).wait_send()


def sum_all(n, factor, dprojt, normed, cott, actt, w_in):
    gi, go, width = dprojt.shape[1], cott.shape[1], normed.shape[1]
    units = actt.shape[0]
    rows = gi + go
    rows_x = rows * 7 // 15 // 32 * 32
    rows_r, rows_h, cols = rows - rows_x, rows_x // 2, width // 2
    vmem = pl.BlockSpec(memory_space=pltpu.VMEM)
    f32 = jnp.float32
    dma = pltpu.SemaphoreType.DMA
    tokens = normed.shape[0] // 2
    return pl.pallas_call(
        functools.partial(sum_kernel, n, factor),
        out_shape=(
            jax.ShapeDtypeStruct((2, gi, width), f32),
            jax.ShapeDtypeStruct((go, 2 * units), f32),
            jax.ShapeDtypeStruct((tokens, width), jnp.bfloat16),
        ),
        in_specs=[vmem] * 4 + [pl.BlockSpec(memory_space=pl.ANY)],
        out_specs=(vmem,) * 3,
        scratch_shapes=[
            pltpu.VMEM((2, rows_r, cols), f32),
            pltpu.VMEM((n, 2, rows_h, cols), f32),
            pltpu.VMEM((2, n - 1, rows_r, cols), f32),
            pltpu.VMEM((n, 2, rows_h, cols), f32),
            pltpu.VMEM((2, n - 1, rows_h, cols), f32),
            pltpu.VMEM((2, rows_r, cols), f32),
            pltpu.VMEM((2, rows_r, cols), f32),
            pltpu.VMEM((2, go, cols), f32),
            pltpu.VMEM((tokens, width), f32),
            pltpu.VMEM((tokens, width), f32),
            pltpu.VMEM((gi, width), jnp.bfloat16),
            dma((2, 2, n - 1)),
            dma((2, 2, n - 1)),
            dma((2, n)),
            dma((2, 2)),
            dma((2, 2)),
            dma((2, 2)),
            dma((2, 3, 2)),
            dma((2,)),
            dma,
        ],
        compiler_params=pltpu.CompilerParams(
            collective_id=1, has_side_effects=True, vmem_limit_bytes=62 * 2**20
        ),
        cost_estimate=pl.CostEstimate(
            flops=6 * n * rows * tokens * width, bytes_accessed=20 * 2**20, transcendentals=0
        ),
        name="sum_gradients",
    )(dprojt, normed, cott, actt, w_in)


def local(normed, w_in, w_out, cotangent):
    width = w_out.shape[1]
    model = w_in.shape[1]
    n = lax.axis_size("dp")
    outer = lax.axis_size("grp")
    tokens = normed.shape[0]
    factor = (tokens * n * outer) ** (-0.5)
    core = lax.rem(lax.axis_index("grp"), 2)
    gi = 2 * width // n // 2
    go = model // n
    units = width // 2

    w_in_c = lax.dynamic_index_in_dim(
        w_in.reshape(n, 2, gi, model), core, 1, keepdims=False
    )
    w_out_c = lax.dynamic_index_in_dim(
        w_out.T.reshape(n // 2, 2, gi, model), core, 1, keepdims=False
    ).reshape(units, model)

    both, both_cot = trade(normed, cotangent)
    projt = lax.dot_general(
        w_in_c.reshape(2 * units, model), both, (((1,), (1,)), ((), ())),
        preferred_element_type=jnp.float32,
    )
    value, gate = projt[:units], projt[units:]
    cdf = 0.5 * (1.0 + lax.erf(gate * 2.0 ** (-0.5)))
    density = jnp.exp(-0.5 * gate * gate) * (2.0 * jnp.pi) ** (-0.5)
    actt = (value * gate * cdf).astype(jnp.bfloat16)
    dactt = lax.dot_general(
        w_out_c, both_cot, (((1,), (1,)), ((), ())), preferred_element_type=jnp.float32
    )
    d_value = dactt * gate * cdf
    d_gate = dactt * value * (cdf + gate * density)
    dprojt = jnp.concatenate([d_value, d_gate], axis=0).astype(jnp.bfloat16)

    grad_in, grad_out, grad_normed = sum_all(
        n, factor, dprojt.reshape(n, gi, 2 * tokens), both,
        both_cot.T.reshape(n, go, 2 * tokens), actt, w_in_c,
    )
    return (grad_in.reshape(2 * gi, model), grad_out, grad_normed)


def solution(mesh):
    placed = (P(("grp", "dp"), None), P(), P(), P(("grp", "dp"), None))
    return jax.shard_map(
        local,
        mesh=mesh,
        in_specs=placed,
        out_specs=(P("dp", None), P("dp", None), P(("grp", "dp"), None)),
        check_vma=False,
    )
```

time: 277 us -> 250 us (0.903)
  local copies, waits for them, and re-layouts: 48.3 us -> 28.8 us
  other arithmetic: 16.9 us -> 5.45 us
  Pallas kernels: 186 us -> 193 us
    convert_element_type x3 -> x0, other arithmetic: 15 us -> none  [the longest x1 5.82 us: local(): actt = (value * gate * cdf).astype(jnp.bfloat16)]
    transpose x3 -> x0, local copies, waits for them, and re-layouts: 10.8 us -> none  [the longest x1 4.47 us: local(): wide_r[:, :go].reshape(2, go, n // 2, gi).transpose(1, 2, 0, 3)]
    reshape x3 -> x0, local copies, waits for them, and re-layouts: 10.4 us -> none  [the longest x2 6.37 us: local(): wide_r[:, :go].reshape(2, go, n // 2, gi).transpose(1, 2, 0, 3)]
    pallas_call x1, Pallas kernels: 177 us -> 183 us  [sum_all(): pl.pallas_call(functools.partial(sum_kernel, n, factor), out_shape=(jax.S...]
    slice x3 -> x0, local copies, waits for them, and re-layouts: 5.88 us -> none  [the longest x2 4.15 us: local(): wide_r[:, go:]]
    unnamed x21 -> x22, local copies, waits for them, and re-layouts: 13.1 us -> 17.3 us
    concatenate x1, other arithmetic: 1.92 us -> 5.45 us  [local(): dprojt = jnp.concatenate([d_value, d_gate], axis=0).astype(jnp.bfloat16)]
    squeeze x0 -> x1, local copies, waits for them, and re-layouts: none -> 3.11 us  [local(): lax.dynamic_index_in_dim(w_in.reshape(n, 2, gi, model), core, 1, keepdims...]
  transfers between devices with their start and end apart: 1 -> 0, of which waited for: 0 -> 0; matrix products, arithmetic and copies ran while one was open for 15% -> 0% of each run, Pallas kernels for 64% -> 0%
where the time goes in v2:
time: 250 us; the launch traced here: 249 us
  Pallas kernels  193 us (77%)
  local copies, waits for them, and re-layouts  28.8 us (12%)
  matrix products  21.8 us (9%)
  other arithmetic  5.45 us (2%)
    pallas_call x1, Pallas kernels, sum_all(): pl.pallas_call(functools.partial(sum_kernel, n, factor), out_shape=(jax.S...  183 us
    unnamed x22, local copies, waits for them, and re-layouts  17.3 us
    dot_general x1, matrix products, local(): lax.dot_general(w_out_c, both_cot, (((1,), (1,)), ((), ())), preferred_el...  12 us
    dot_general x1, matrix products, local(): lax.dot_general(w_in_c.reshape(2 * units, model), both, (((1,), (1,)), ((...  9.83 us
    pallas_call x1, Pallas kernels, trade(): pl.pallas_call(trade_kernel, out_shape=(whole, whole), in_specs=[vmem, vm...  9.16 us
    concatenate x1, other arithmetic, local(): dprojt = jnp.concatenate([d_value, d_gate], axis=0).astype(jnp.bfloat16)  5.45 us

profile of v2, /device:TPU:1, one launch (start us, length us, event | category | flops | bytes accessed | tf_op | source)
XLA Modules:
  0.0 249.4 jit_solution(8030788656866789332)
XLA Ops:
  0.6 0.0 copy-start
  0.6 0.0 copy-start.1
  0.7 3.5 %constant_dynamic-slice_fusion = bf16[8,1,320,1280]{3,2,1,0:T(8,128)(2,1)S(1)} fusion(bf16[8,2,320,1280]{3,2,1,0:T(8,128)(2,1)} %bitcast.21, s32[]{:T(128)S(6)} %select_n.6), kind=kLoop, calls=%fused_computation.11 | loop fusion | bytes 13107204 | tf_op jit(solution)/shard_map/jit(dynamic_index_in_dim)/dynamic_slice | solution.py:357
  4.1 0.0 copy-done
  4.1 0.1 copy-done.1
  4.2 9.2 %trade_tokens.1 = (bf16[1024,1280]{1,0:T(8,128)(2,1)S(1)}, bf16[1024,1280]{1,0:T(8,128)(2,1)S(1)}) custom-call(bf16[512,1280]{1,0:T(8,128)(2,1)S(1)} %copy-done, bf16[512,1280]{1,0:T(8,128)(2,1)S(1)} %copy-done.1), custom_call_target="tpu_custom_call" | custom-call | tf_op jit(solution)/shard_map/trade_tokens/pallas_call | solution.py:51
  13.4 0.0 copy-start.2
  13.4 1.5 copy-done.2
  14.9 9.8 %fusion.6 = f32[2560,1024]{1,0:T(8,128)} fusion(bf16[2560,1280]{1,0:T(8,128)(2,1)S(1)} %bitcast.25, bf16[1024,1280]{1,0:T(8,128)(2,1)S(1)} %get-tuple-element.9.normed), kind=kOutput, calls=%fused_computation.13 | convolution fusion | flops 6710886400 | bytes 19660800 | tf_op jit(solution)/shard_map/dot_general | solution.py:365
  24.7 9.4 %copy.9 = bf16[1280,2560]{0,1:T(8,128)(2,1)} copy(bf16[1280,2560]{1,0:T(8,128)(2,1)} %param.6) | data formatting | bytes 13107200 | tf_op args[2]
  34.2 0.0 slice-start
  34.2 2.3 constant_dynamic-slice_fusion.1
  36.5 0.0 slice-start.1
  36.5 0.0 slice-start.2
  36.5 0.0 slice-start.3
  36.5 12.0 %multiply_convert_fusion.1 = (bf16[1280,1024]{1,0:T(8,128)(2,1)}, bf16[1280,1024]{1,0:T(8,128)(2,1)}, bf16[1280,1024]{1,0:T(8,128)(2,1)}) fusion(f32[2560,1024]{1,0:T(8,128)} %fusion.6, bf16[1280,1280]{1,0:T(8,128)(2,1)S(1)} %bitcast.28, bf16[1024,1280]{1,0:T(8,128)(2,1)S(1)} %get-tuple-element.8), kind=kOutput, calls=%fused_computation.9 | convolution fusion | flops 3377725440 | bytes 24248320 | tf_op jit(solution)/shard_map/dot_general | solution.py:373
  48.5 5.4 %pad_maximum_fusion = bf16[2560,1024]{1,0:T(8,128)(2,1)} fusion(bf16[1280,1024]{1,0:T(8,128)(2,1)} %get-tuple-element.14, bf16[1280,1024]{1,0:T(8,128)(2,1)} %get-tuple-element.13), kind=kLoop, calls=%fused_computation.7 | loop fusion | flops 10485760 | bytes 10485760 | tf_op jit(solution)/shard_map/concatenate | solution.py:378
  53.9 0.0 slice-done
  53.9 0.0 slice-done.1
  53.9 0.0 slice-done.2
  53.9 0.0 slice-done.3
  53.9 3.1 %fusion.11.w_in = bf16[8,320,1280]{2,1,0:T(8,128)(2,1)} fusion(bf16[8,2,320,1280]{3,2,1,0:T(8,128)(2,1)S(1)} %bitcast.24, s32[]{:T(128)S(6)} %select_n.6), kind=kLoop, calls=%fused_computation.14 | loop fusion | bytes 13107204 | tf_op jit(solution)/shard_map/jit(dynamic_index_in_dim)/squeeze | solution.py:357
  57.1 2.6 %copy.11 = bf16[1280,1024]{1,0:T(8,128)(2,1)} copy(bf16[1280,1024]{0,1:T(8,128)(2,1)S(1)} %bitcast.19) | data formatting | bytes 5242880 | tf_op jit(solution)/shard_map/transpose | solution.py:382
  59.7 183.5 %sum_gradients.1 = (f32[2,320,1280]{2,1,0:T(8,128)}, f32[160,2560]{1,0:T(8,128)}, bf16[512,1280]{1,0:T(8,128)(2,1)}) custom-call(bf16[8,320,1024]{2,1,0:T(8,128)(2,1)} %bitcast.26, bf16[1024,1280]{1,0:T(8,128)(2,1)} %copy-done.2, bf16[8,160,1024]{2,1,0:T(8,128)(2,1)} %bitcast.29, bf16[1280,1024]{1,0:T(8,128)(2,1)} %get-tuple-element.15.actt, ...), custom_call_target="tpu_custom_call" | custom-call | flops 15099494400 | bytes 20971520 | tf_op jit(solution)/shard_map/sum_gradients/pallas_call | solution.py:304
  243.2 0.0 copy-start.3
  243.2 0.0 copy-start.4
  243.2 4.0 %copy.16 = f32[640,1280]{1,0:T(8,128)} copy(f32[640,1280]{1,0:T(8,128)} %bitcast.27) | data formatting | bytes 6553600
  247.2 0.0 copy-done.3
  247.2 1.2 copy.17
  248.3 0.0 copy-done.4
  248.4 1.1 copy.18
  (1 shorter events, 0.0 us)
Async XLA Ops:
  0.6 3.5 %copy-start = (bf16[512,1280]{1,0:T(8,128)(2,1)S(1)}, bf16[512,1280]{1,0:T(8,128)(2,1)}, u32[]{:S(2)}) copy-start(bf16[512,1280]{1,0:T(8,128)(2,1)} %normed.1) | copy-start | bytes 3932164
  0.6 3.6 %copy-start.1 = (bf16[512,1280]{1,0:T(8,128)(2,1)S(1)}, bf16[512,1280]{1,0:T(8,128)(2,1)}, u32[]{:S(2)}) copy-start(bf16[512,1280]{1,0:T(8,128)(2,1)} %cot.1) | copy-start | bytes 3932164
  13.4 1.5 copy-start.2
  34.2 19.7 %slice-start = ((s8[13107200]{0:T(1024)(128)(4,1)}), s8[4194304]{0:T(1024)(128)(4,1)S(1)}, s32[]{:S(2)}) async-start(s8[13107200]{0:T(1024)(128)(4,1)} %bitcast.22), calls=%async_computation | async-start | bytes 8388608
  36.5 17.4 %slice-start.1 = ((s8[13107200]{0:T(1024)(128)(4,1)}), s8[4194304]{0:T(1024)(128)(4,1)S(1)}, s32[]{:S(2)}) async-start(s8[13107200]{0:T(1024)(128)(4,1)} %bitcast.22), calls=%async_computation.1 | async-start | bytes 8388608
  36.5 17.4 %slice-start.2 = ((s8[13107200]{0:T(1024)(128)(4,1)}), s8[4194304]{0:T(1024)(128)(4,1)S(1)}, s32[]{:S(2)}) async-start(s8[13107200]{0:T(1024)(128)(4,1)} %bitcast.22), calls=%async_computation.2 | async-start | bytes 8388608
  36.5 17.4 %slice-start.3 = ((s8[13107200]{0:T(1024)(128)(4,1)}), s8[524288]{0:T(1024)(128)(4,1)S(1)}, s32[]{:S(2)}) async-start(s8[13107200]{0:T(1024)(128)(4,1)} %bitcast.22), calls=%async_computation.3 | async-start | bytes 1048576
  243.2 4.0 %copy-start.3 = (f32[160,2560]{1,0:T(8,128)S(1)}, f32[160,2560]{1,0:T(8,128)}, u32[]{:S(2)}) copy-start(f32[160,2560]{1,0:T(8,128)} %get-tuple-element.20) | copy-start | bytes 4915204
  243.2 5.2 %copy-start.4 = (bf16[512,1280]{1,0:T(8,128)(2,1)S(1)}, bf16[512,1280]{1,0:T(8,128)(2,1)}, u32[]{:S(2)}) copy-start(bf16[512,1280]{1,0:T(8,128)(2,1)} %get-tuple-element.21) | copy-start | bytes 3932164

commit v3 on v2

--- a/solution.py
+++ b/solution.py
@@ -17,13 +17,24 @@
     pl.semaphore_wait(barrier, len(partners))
 
 
-def trade_kernel(normed, cot, all_normed, all_cot, mine, theirs, send_sem, recv_sem):
+def head_kernel(
+    n, normed, cot, w_out, w_in, all_normed, cott, dprojt, actt,
+    mine, theirs, w_now, w_outt, send_sem, recv_sem, fetch,
+):
     grp = lax.axis_index("grp")
     dp = lax.axis_index("dp")
-    other = (grp + 1 - 2 * lax.rem(grp, 2), dp)
-    rows = normed.shape[0]
-    mine[0] = normed[...].astype(jnp.float32)
-    mine[1] = cot[...].astype(jnp.float32)
+    core = lax.rem(grp, 2)
+    other = (grp + 1 - 2 * core, dp)
+    rows, model = normed.shape
+    gi, go = dprojt.shape[1], cott.shape[1]
+    half = n // 2
+    loads = [
+        pltpu.make_async_copy(w_in.at[d, core], w_now.at[d], fetch.at[d]) for d in range(n)
+    ]
+    for load in loads:
+        load.start()
+    mine[0] = cot[...].astype(jnp.float32)
+    mine[1] = normed[...].astype(jnp.float32)
     greet([other])
     copies = [
         pltpu.make_async_remote_copy(
@@ -34,36 +45,78 @@
     ]
     for copy in copies:
         copy.start()
+    step = w_out.shape[1] // 4
+    for j in range(4):
+        part = slice(j * step, (j + 1) * step)
+        w_outt[part, :] = w_out[:, part].T
     all_normed[:rows] = normed[...]
-    all_cot[:rows] = cot[...]
+    turned = cot[...].T
+    for d in range(n):
+        cott[d, :, :rows] = turned[d * go : (d + 1) * go]
     copies[0].wait_recv()
-    all_normed[rows:] = theirs[0].astype(jnp.bfloat16)
+    turned = theirs[0].T.astype(jnp.bfloat16)
+    for d in range(n):
+        cott[d, :, rows:] = turned[d * go : (d + 1) * go]
     copies[1].wait_recv()
-    all_cot[rows:] = theirs[1].astype(jnp.bfloat16)
+    all_normed[rows:] = theirs[1].astype(jnp.bfloat16)
+    for load in loads:
+        load.wait()
+
+    def dot(left, right, axis):
+        return lax.dot_general(
+            left, right, (((1,), (axis,)), ((), ())), preferred_element_type=jnp.float32
+        )
+
+    tokens_t = cott[...].reshape(model, 2 * rows)
+
+    def block(b, carry):
+        value = dot(w_now[b], all_normed[...], 1)
+        gate = dot(w_now[b + half], all_normed[...], 1)
+        units = pl.ds(pl.multiple_of((2 * b + core) * gi, 16), gi)
+        dact = dot(w_outt[units, :], tokens_t, 0)
+        cdf = 0.5 * (1.0 + lax.erf(gate * 2.0 ** (-0.5)))
+        density = jnp.exp(-0.5 * gate * gate) * (2.0 * jnp.pi) ** (-0.5)
+        gelu = gate * cdf
+        actt[pl.ds(pl.multiple_of(b * gi, 16), gi), :] = (value * gelu).astype(jnp.bfloat16)
+        dprojt[b] = (dact * gelu).astype(jnp.bfloat16)
+        dprojt[b + half] = (dact * value * (cdf + gate * density)).astype(jnp.bfloat16)
+        return carry
+
+    lax.fori_loop(0, half, block, 0)
     for copy in copies:
         copy.wait_send()
 
 
-def trade(normed, cot):
-    rows, width = normed.shape
-    whole = jax.ShapeDtypeStruct((2 * rows, width), jnp.bfloat16)
+def make_terms(n, normed, cot, w_out, w_in):
+    rows, model = normed.shape
+    gi, width = w_in.shape[2], w_out.shape[1]
+    go = model // n
+    bf16 = jnp.bfloat16
     vmem = pl.BlockSpec(memory_space=pltpu.VMEM)
     return pl.pallas_call(
-        trade_kernel,
-        out_shape=(whole, whole),
-        in_specs=[vmem, vmem],
-        out_specs=(vmem, vmem),
+        functools.partial(head_kernel, n),
+        out_shape=(
+            jax.ShapeDtypeStruct((2 * rows, model), bf16),
+            jax.ShapeDtypeStruct((n, go, 2 * rows), bf16),
+            jax.ShapeDtypeStruct((n, gi, 2 * rows), bf16),
+            jax.ShapeDtypeStruct((width // 2, 2 * rows), bf16),
+        ),
+        in_specs=[vmem] * 3 + [pl.BlockSpec(memory_space=pl.ANY)],
+        out_specs=(vmem,) * 4,
         scratch_shapes=[
-            pltpu.VMEM((2, rows, width), jnp.float32),
-            pltpu.VMEM((2, rows, width), jnp.float32),
+            pltpu.VMEM((2, rows, model), jnp.float32),
+            pltpu.VMEM((2, rows, model), jnp.float32),
+            pltpu.VMEM((n, gi, model), bf16),
+            pltpu.VMEM((width, model), bf16),
             pltpu.SemaphoreType.DMA((2,)),
             pltpu.SemaphoreType.DMA((2,)),
+            pltpu.SemaphoreType.DMA((n,)),
         ],
         compiler_params=pltpu.CompilerParams(
-            collective_id=0, has_side_effects=True, vmem_limit_bytes=40 * 2**20
+            collective_id=0, has_side_effects=True, vmem_limit_bytes=60 * 2**20
         ),
-        name="trade_tokens",
-    )(normed, cot)
+        name="make_terms",
+    )(normed, cot, w_out, w_in)
 
 
 def sum_kernel(
@@ -154,7 +207,7 @@
     tokens = out_normed.shape[0]
 
     def add_share(d, k, total):
-        copy = pltpu.make_async_copy(w_in.at[d], w_now, fetch)
+        copy = pltpu.make_async_copy(w_in.at[d, core], w_now, fetch)
         copy.start()
         copy.wait()
         rows = slice(k * tokens, (k + 1) * tokens)
@@ -349,38 +402,10 @@
     outer = lax.axis_size("grp")
     tokens = normed.shape[0]
     factor = (tokens * n * outer) ** (-0.5)
-    core = lax.rem(lax.axis_index("grp"), 2)
-    gi = 2 * width // n // 2
-    go = model // n
-    units = width // 2
-
-    w_in_c = lax.dynamic_index_in_dim(
-        w_in.reshape(n, 2, gi, model), core, 1, keepdims=False
-    )
-    w_out_c = lax.dynamic_index_in_dim(
-        w_out.T.reshape(n // 2, 2, gi, model), core, 1, keepdims=False
-    ).reshape(units, model)
-
-    both, both_cot = trade(normed, cotangent)
-    projt = lax.dot_general(
-        w_in_c.reshape(2 * units, model), both, (((1,), (1,)), ((), ())),
-        preferred_element_type=jnp.float32,
-    )
-    value, gate = projt[:units], projt[units:]
-    cdf = 0.5 * (1.0 + lax.erf(gate * 2.0 ** (-0.5)))
-    density = jnp.exp(-0.5 * gate * gate) * (2.0 * jnp.pi) ** (-0.5)
-    actt = (value * gate * cdf).astype(jnp.bfloat16)
-    dactt = lax.dot_general(
-        w_out_c, both_cot, (((1,), (1,)), ((), ())), preferred_element_type=jnp.float32
-    )
-    d_value = dactt * gate * cdf
-    d_gate = dactt * value * (cdf + gate * density)
-    dprojt = jnp.concatenate([d_value, d_gate], axis=0).astype(jnp.bfloat16)
-
-    grad_in, grad_out, grad_normed = sum_all(
-        n, factor, dprojt.reshape(n, gi, 2 * tokens), both,
-        both_cot.T.reshape(n, go, 2 * tokens), actt, w_in_c,
-    )
+    gi = width // n
+    blocks = w_in.reshape(n, 2, gi, model)
+    both, cott, dprojt, actt = make_terms(n, normed, cotangent, w_out, blocks)
+    grad_in, grad_out, grad_normed = sum_all(n, factor, dprojt, both, cott, actt, blocks)
     return (grad_in.reshape(2 * gi, model), grad_out, grad_normed)
 
 

time: 250 us -> 221 us (0.88)
  local copies, waits for them, and re-layouts: 28.8 us -> 6.93 us
  matrix products: 21.8 us -> 0 us
  Pallas kernels: 193 us -> 213 us
  other arithmetic: 5.45 us -> 0 us
    dot_general x2 -> x0, matrix products: 21.8 us -> none  [the longest x1 12 us: local(): lax.dot_general(w_out_c, both_cot, (((1,), (1,)), ((), ())), preferred_el...]
    pallas_call x1, Pallas kernels: 9.16 us -> 29.5 us  [make_terms(): pl.pallas_call(functools.partial(head_kernel, n), out_shape=(jax.ShapeDty...]
    unnamed x22 -> x7, local copies, waits for them, and re-layouts: 17.3 us -> 6.93 us
    dynamic_slice x2 -> x0, local copies, waits for them, and re-layouts: 5.76 us -> none  [the longest x1 3.47 us: local(): lax.dynamic_index_in_dim(w_in.reshape(n, 2, gi, model), core, 1, keepdims...]
    concatenate x1 -> x0, other arithmetic: 5.45 us -> none  [local(): dprojt = jnp.concatenate([d_value, d_gate], axis=0).astype(jnp.bfloat16)]
    squeeze x1 -> x0, local copies, waits for them, and re-layouts: 3.11 us -> none  [local(): lax.dynamic_index_in_dim(w_in.reshape(n, 2, gi, model), core, 1, keepdims...]
    transpose x1 -> x0, local copies, waits for them, and re-layouts: 2.61 us -> none  [local(): both_cot.T.reshape(n, go, 2 * tokens)]
where the time goes in v3:
time: 221 us; the launch traced here: 220 us
  Pallas kernels  213 us (96%)
  local copies, waits for them, and re-layouts  6.93 us (3%)
    pallas_call x1, Pallas kernels, sum_all(): pl.pallas_call(functools.partial(sum_kernel, n, factor), out_shape=(jax.S...  183 us
    pallas_call x1, Pallas kernels, make_terms(): pl.pallas_call(functools.partial(head_kernel, n), out_shape=(jax.ShapeDty...  29.5 us
    unnamed x7, local copies, waits for them, and re-layouts  6.93 us

profile of v3, /device:TPU:1, one launch (start us, length us, event | category | flops | bytes accessed | tf_op | source)
XLA Modules:
  0.0 220.4 jit_solution(11749733558051180680)
XLA Ops:
  0.6 29.5 %make_terms.1 = (bf16[1024,1280]{1,0:T(8,128)(2,1)}, bf16[8,160,1024]{2,1,0:T(8,128)(2,1)}, bf16[8,320,1024]{2,1,0:T(8,128)(2,1)}, bf16[1280,1024]{1,0:T(8,128)(2,1)}) custom-call(bf16[512,1280]{1,0:T(8,128)(2,1)} %normed.1, bf16[512,1280]{1,0:T(8,128)(2,1)} %cot.1, bf16[1280,2560]{1,0:T(8,128)(2,1)} %w_out.1, bf16[8,2,320,1280]{3,2,1,0:T(8,128)(2,1)} %bitcast.2), custom_call_target="tpu_custom_call" | custom-call | tf_op jit(solution)/shard_map/make_terms/pallas_call | solution.py:96
  30.1 183.3 %sum_gradients.1 = (f32[2,320,1280]{2,1,0:T(8,128)}, f32[160,2560]{1,0:T(8,128)}, bf16[512,1280]{1,0:T(8,128)(2,1)}) custom-call(bf16[8,320,1024]{2,1,0:T(8,128)(2,1)} %get-tuple-element.10.dprojt, bf16[1024,1280]{1,0:T(8,128)(2,1)} %get-tuple-element.11.normed, bf16[8,160,1024]{2,1,0:T(8,128)(2,1)} %get-tuple-element.12.cott, ...), custom_call_target="tpu_custom_call" | custom-call | flops 15099494400 | bytes 20971520 | tf_op jit(solution)/shard_map/sum_gradients/pallas_call | solution.py:357
  213.4 0.0 copy-start
  213.5 4.0 %copy.10 = f32[640,1280]{1,0:T(8,128)} copy(f32[640,1280]{1,0:T(8,128)} %bitcast.4) | data formatting | bytes 6553600
  217.4 0.0 copy-done
  217.4 0.0 copy-start.1
  217.4 1.2 copy.11
  218.6 0.7 copy-done.1
  219.3 1.1 copy.12
Async XLA Ops:
  213.4 4.0 %copy-start = (f32[160,2560]{1,0:T(8,128)S(1)}, f32[160,2560]{1,0:T(8,128)}, u32[]{:S(2)}) copy-start(f32[160,2560]{1,0:T(8,128)} %get-tuple-element.21) | copy-start | bytes 4915204
  217.4 1.9 copy-start.1

commit v4 on v3

--- a/solution.py
+++ b/solution.py
@@ -174,13 +174,20 @@
             recv_sem=sems.at[(1,) + where], device_id=device, device_id_type=MESH,
         )
 
-    def hop_r(way, s, first=False):
-        src = final_r.at[way] if first else land_r.at[way, s - 1]
-        return remote(src, land_r.at[way, s], ring_r, (way, s), onward[way])
-
-    def hop_x(way, s, first=False):
-        src = land_e.at[0, way] if first else land_x.at[way, s - 1]
-        return remote(src, land_x.at[way, s], ring_x, (way, s), onward[way])
+    streams = [(way, k) for k in range(2) for way in range(2)]
+    cut_r, cut_x = rows_r // 16 * 8, rows_h // 16 * 8
+    group_r = (slice(0, cut_r), slice(cut_r, rows_r))
+    group_x = (slice(0, cut_x), slice(cut_x, rows_h))
+
+    def hop_r(way, k, s, first=False):
+        rows = group_r[k]
+        src = final_r.at[way, rows] if first else land_r.at[way, s - 1, rows]
+        return remote(src, land_r.at[way, s, rows], ring_r, (2 * way + k, s), onward[way])
+
+    def hop_x(way, k, s, first=False):
+        rows = group_x[k]
+        src = land_e.at[0, way, rows] if first else land_x.at[way, s - 1, rows]
+        return remote(src, land_x.at[way, s, rows], ring_x, (2 * way + k, s), onward[way])
 
     def give_half(s):
         return remote(part_e.at[s], land_e.at[s], halves, (s,), along_x)
@@ -195,7 +202,8 @@
     for way in range(2):
         compute_r(way, 0)
         final_r[way] = part_r[way]
-        hop_r(way, 0, True).start()
+    for way, k in streams:
+        hop_r(way, k, 0, True).start()
 
     def make_x(s):
         for way in range(2):
@@ -222,10 +230,11 @@
     def step_r(s):
         for way in range(2):
             compute_r(way, s + 1)
-        for way in range(2):
-            hop_r(way, s, True).wait_recv()
-            land_r[way, s] = land_r[way, s] + part_r[way]
-            hop_r(way, s + 1).start()
+        for way, k in streams:
+            hop_r(way, k, s, True).wait_recv()
+            rows = group_r[k]
+            land_r[way, s, rows] = land_r[way, s, rows] + part_r[way, rows]
+            hop_r(way, k, s + 1).start()
 
     def step_first(s):
         step_r(s)
@@ -238,10 +247,11 @@
         give_half(s + 1).wait_recv()
         for way in range(2):
             land_e[s + 1, way] = own_x(way, s + 1)
-        for way in range(2):
-            hop_x(way, s, True).wait_recv()
-            land_x[way, s] = land_x[way, s] + land_e[s + 1, way]
-            hop_x(way, s + 1).start()
+        for way, k in streams:
+            hop_x(way, k, s, True).wait_recv()
+            rows = group_x[k]
+            land_x[way, s, rows] = land_x[way, s, rows] + land_e[s + 1, way, rows]
+            hop_x(way, k, s + 1).start()
 
     def step_both(s):
         step_r(s)
@@ -257,7 +267,8 @@
     give_half(0).wait_recv()
     for way in range(2):
         land_e[0, way] = own_x(way, 0)
-        hop_x(way, 0, True).start()
+    for way, k in streams:
+        hop_x(way, k, 0, True).start()
     loop(lag, n - 2, step_both)
 
     out_normed[...] = land_s[...].astype(out_normed.dtype)
@@ -267,7 +278,8 @@
 
     for way in range(2):
         compute_r(way, n - 1)
-        hop_r(way, n - 2, True).wait_recv()
+        for k in range(2):
+            hop_r(way, k, n - 2, True).wait_recv()
         part_r[way] = (land_r[way, n - 2] + part_r[way]) * factor
         swap_r(way).start()
 
@@ -280,32 +292,36 @@
     def tell_o(way):
         return remote(final_r.at[way, :go], land_o.at[way], core_o, (way,), other)
 
-    def show(which, c, h, way, device):
-        rows = pl.ds(pl.multiple_of(split + h * rows_h, 8), rows_h)
-        spot = out_in.at[c, rows, spans[way]]
-        return remote(spot, spot, spread, (which, way), device)
+    def x_rows(h, k):
+        start = split + h * rows_h + group_x[k].start
+        return pl.ds(pl.multiple_of(start, 8), group_x[k].stop - group_x[k].start)
+
+    def show(which, c, h, way, k, device):
+        spot = out_in.at[c, x_rows(h, k), spans[way]]
+        return remote(spot, spot, spread, (which, 2 * way + k), device)
 
     give_half(n - 1).wait_recv()
     for way in range(2):
         land_e[n - 1, way] = own_x(way, n - 1)
-    rows_x = pl.ds(pl.multiple_of(split + x * rows_h, 8), rows_h)
-    for way in range(2):
-        hop_x(way, n - 2, True).wait_recv()
-        out_in[core, rows_x, spans[way]] = (
-            land_x[way, n - 2] + land_e[n - 1, way]
+    for way, k in streams:
+        hop_x(way, k, n - 2, True).wait_recv()
+        rows = group_x[k]
+        out_in[core, x_rows(x, k), spans[way]] = (
+            land_x[way, n - 2, rows] + land_e[n - 1, way, rows]
         ) * factor
-        show(0, core, x, way, along_x).start()
-        show(1, core, x, way, other).start()
+        show(0, core, x, way, k, along_x).start()
+        show(1, core, x, way, k, other).start()
     for way in range(2):
         swap_r(way).wait_recv()
-        hop_r(way, 0, True).wait_send()
+        for k in range(2):
+            hop_r(way, k, 0, True).wait_send()
         final_r[way, :go] = part_r[way, :go] + land_p[way, :go]
         tell_o(way).start()
         out_in[core, :split, spans[way]] = part_r[way, go:] + land_p[way, go:]
         tell_r(core, way).start()
-    for way in range(2):
-        show(0, core, 1 - x, way, along_x).wait_recv()
-        show(2, core, 1 - x, way, other).start()
+    for way, k in streams:
+        show(0, core, 1 - x, way, k, along_x).wait_recv()
+        show(2, core, 1 - x, way, k, other).start()
     for way in range(2):
         tell_o(way).wait_recv()
     mine = jnp.concatenate([final_r[0, :go], final_r[1, :go]], axis=1)
@@ -322,26 +338,28 @@
     )
     for way in range(2):
         tell_r(1 - core, way).wait_recv()
-        show(1, 1 - core, x, way, other).wait_recv()
-        show(2, 1 - core, 1 - x, way, other).wait_recv()
+    for way, k in streams:
+        show(1, 1 - core, x, way, k, other).wait_recv()
+        show(2, 1 - core, 1 - x, way, k, other).wait_recv()
 
     def drain(s):
-        for way in range(2):
-            hop_r(way, s + 1).wait_send()
-            hop_x(way, s, True).wait_send()
+        for way, k in streams:
+            hop_r(way, k, s + 1).wait_send()
+            hop_x(way, k, s, True).wait_send()
 
     loop(0, n - 2, drain)
-    for way in range(2):
-        hop_x(way, n - 2, True).wait_send()
+    for way, k in streams:
+        hop_x(way, k, n - 2, True).wait_send()
     loop(0, n, lambda s: give_half(s).wait_send())
     give_share.wait_send()
     for way in range(2):
         swap_r(way).wait_send()
         tell_o(way).wait_send()
         tell_r(core, way).wait_send()
-        show(0, core, x, way, along_x).wait_send()
-        show(1, core, x, way, other).wait_send()
-        show(2, core, 1 - x, way, other).wait_send()
+    for way, k in streams:
+        show(0, core, x, way, k, along_x).wait_send()
+        show(1, core, x, way, k, other).wait_send()
+        show(2, core, 1 - x, way, k, other).wait_send()
 
 
 def sum_all(n, factor, dprojt, normed, cott, actt, w_in):
@@ -375,13 +393,13 @@
             pltpu.VMEM((tokens, width), f32),
             pltpu.VMEM((tokens, width), f32),
             pltpu.VMEM((gi, width), jnp.bfloat16),
-            dma((2, 2, n - 1)),
-            dma((2, 2, n - 1)),
+            dma((2, 4, n - 1)),
+            dma((2, 4, n - 1)),
             dma((2, n)),
             dma((2, 2)),
             dma((2, 2)),
             dma((2, 2)),
-            dma((2, 3, 2)),
+            dma((2, 3, 4)),
             dma((2,)),
             dma,
         ],

time: 221 us -> 216 us (0.977)
  Pallas kernels: 213 us -> 207 us
    pallas_call x1, Pallas kernels: 183 us -> 178 us  [sum_all(): pl.pallas_call(functools.partial(sum_kernel, n, factor), out_shape=(jax.S...]
where the time goes in v4:
time: 216 us; the launch traced here: 215 us
  Pallas kernels  207 us (96%)
  local copies, waits for them, and re-layouts  6.93 us (3%)
    pallas_call x1, Pallas kernels, sum_all(): pl.pallas_call(functools.partial(sum_kernel, n, factor), out_shape=(jax.S...  178 us
    pallas_call x1, Pallas kernels, make_terms(): pl.pallas_call(functools.partial(head_kernel, n), out_shape=(jax.ShapeDty...  29.5 us
    unnamed x7, local copies, waits for them, and re-layouts  6.93 us

profile of v4, /device:TPU:1, one launch (start us, length us, event | category | flops | bytes accessed | tf_op | source)
XLA Modules:
  0.0 215.1 jit_solution(4917441839401196939)
XLA Ops:
  0.6 29.5 %make_terms.1 = (bf16[1024,1280]{1,0:T(8,128)(2,1)}, bf16[8,160,1024]{2,1,0:T(8,128)(2,1)}, bf16[8,320,1024]{2,1,0:T(8,128)(2,1)}, bf16[1280,1024]{1,0:T(8,128)(2,1)}) custom-call(bf16[512,1280]{1,0:T(8,128)(2,1)} %normed.1, bf16[512,1280]{1,0:T(8,128)(2,1)} %cot.1, bf16[1280,2560]{1,0:T(8,128)(2,1)} %w_out.1, bf16[8,2,320,1280]{3,2,1,0:T(8,128)(2,1)} %bitcast.2), custom_call_target="tpu_custom_call" | custom-call | tf_op jit(solution)/shard_map/make_terms/pallas_call | solution.py:96
  30.1 178.0 %sum_gradients.1 = (f32[2,320,1280]{2,1,0:T(8,128)}, f32[160,2560]{1,0:T(8,128)}, bf16[512,1280]{1,0:T(8,128)(2,1)}) custom-call(bf16[8,320,1024]{2,1,0:T(8,128)(2,1)} %get-tuple-element.10.dprojt, bf16[1024,1280]{1,0:T(8,128)(2,1)} %get-tuple-element.11.normed, bf16[8,160,1024]{2,1,0:T(8,128)(2,1)} %get-tuple-element.12.cott, ...), custom_call_target="tpu_custom_call" | custom-call | flops 15099494400 | bytes 20971520 | tf_op jit(solution)/shard_map/sum_gradients/pallas_call | solution.py:375
  208.1 0.0 copy-start
  208.1 4.0 %copy.10 = f32[640,1280]{1,0:T(8,128)} copy(f32[640,1280]{1,0:T(8,128)} %bitcast.4) | data formatting | bytes 6553600
  212.1 0.0 copy-done
  212.1 0.0 copy-start.1
  212.1 1.2 copy.11
  213.3 0.7 copy-done.1
  214.0 1.1 copy.12
Async XLA Ops:
  208.1 4.0 %copy-start = (f32[160,2560]{1,0:T(8,128)S(1)}, f32[160,2560]{1,0:T(8,128)}, u32[]{:S(2)}) copy-start(f32[160,2560]{1,0:T(8,128)} %get-tuple-element.21) | copy-start | bytes 4915204
  212.1 1.9 copy-start.1

commit v5 on v4

--- a/solution.py
+++ b/solution.py
@@ -366,7 +366,7 @@
     gi, go, width = dprojt.shape[1], cott.shape[1], normed.shape[1]
     units = actt.shape[0]
     rows = gi + go
-    rows_x = rows * 7 // 15 // 32 * 32
+    rows_x = rows * 8 // 15 // 32 * 32
     rows_r, rows_h, cols = rows - rows_x, rows_x // 2, width // 2
     vmem = pl.BlockSpec(memory_space=pltpu.VMEM)
     f32 = jnp.float32

time: 216 us -> 212 us (0.981)
  Pallas kernels: 207 us -> 204 us
    pallas_call x1, Pallas kernels: 178 us -> 174 us  [sum_all(): pl.pallas_call(functools.partial(sum_kernel, n, factor), out_shape=(jax.S...]
where the time goes in v5:
time: 212 us
  Pallas kernels  204 us (96%)
  local copies, waits for them, and re-layouts  6.93 us (3%)
    pallas_call x1, Pallas kernels, sum_all(): pl.pallas_call(functools.partial(sum_kernel, n, factor), out_shape=(jax.S...  174 us
    pallas_call x1, Pallas kernels, make_terms(): pl.pallas_call(functools.partial(head_kernel, n), out_shape=(jax.ShapeDty...  29.5 us
    unnamed x7, local copies, waits for them, and re-layouts  6.93 us

profile of v5, /device:TPU:1, one launch (start us, length us, event | category | flops | bytes accessed | tf_op | source)
XLA Modules:
  0.0 211.5 jit_solution(5310632117980479352)
XLA Ops:
  0.6 29.5 %make_terms.1 = (bf16[1024,1280]{1,0:T(8,128)(2,1)}, bf16[8,160,1024]{2,1,0:T(8,128)(2,1)}, bf16[8,320,1024]{2,1,0:T(8,128)(2,1)}, bf16[1280,1024]{1,0:T(8,128)(2,1)}) custom-call(bf16[512,1280]{1,0:T(8,128)(2,1)} %normed.1, bf16[512,1280]{1,0:T(8,128)(2,1)} %cot.1, bf16[1280,2560]{1,0:T(8,128)(2,1)} %w_out.1, bf16[8,2,320,1280]{3,2,1,0:T(8,128)(2,1)} %bitcast.2), custom_call_target="tpu_custom_call" | custom-call | tf_op jit(solution)/shard_map/make_terms/pallas_call | solution.py:96
  30.1 174.5 %sum_gradients.1 = (f32[2,320,1280]{2,1,0:T(8,128)}, f32[160,2560]{1,0:T(8,128)}, bf16[512,1280]{1,0:T(8,128)(2,1)}) custom-call(bf16[8,320,1024]{2,1,0:T(8,128)(2,1)} %get-tuple-element.10.dprojt, bf16[1024,1280]{1,0:T(8,128)(2,1)} %get-tuple-element.11.normed, bf16[8,160,1024]{2,1,0:T(8,128)(2,1)} %get-tuple-element.12.cott, ...), custom_call_target="tpu_custom_call" | custom-call | flops 15099494400 | bytes 20971520 | tf_op jit(solution)/shard_map/sum_gradients/pallas_call | solution.py:375
  204.6 0.0 copy-start
  204.6 4.0 %copy.10 = f32[640,1280]{1,0:T(8,128)} copy(f32[640,1280]{1,0:T(8,128)} %bitcast.4) | data formatting | bytes 6553600
  208.6 0.0 copy-done
  208.6 0.0 copy-start.1
  208.6 1.2 copy.11
  209.7 0.7 copy-done.1
  210.5 1.1 copy.12
Async XLA Ops:
  204.6 4.0 %copy-start = (f32[160,2560]{1,0:T(8,128)S(1)}, f32[160,2560]{1,0:T(8,128)}, u32[]{:S(2)}) copy-start(f32[160,2560]{1,0:T(8,128)} %get-tuple-element.21) | copy-start | bytes 4915204
  208.6 1.9 copy-start.1
